TPU v7x, 512 devices: a whole 4x8x8 slice. The times are simulated.
512 devices in a mesh: row: 32 (over y, x), col: 16 (over z, core).
Axes of the slice: x: 4, y: 8, z: 8, core: 2. Of those that a mesh axis runs over, the one named last changes fastest.
Arguments:
- top_inverse: float32 [8192, 8192], P('row', 'col'), may hold values from -8 to 8, as said below
- coupling: float32 [2, 8192, 4096], P(None, 'col', 'row'), may hold values from -0.0625 to 0.0625
- child_inverse: float32 [2, 4096, 1024], P(None, 'row'), may hold values from -2 to 2, as said below
- tile_mask: int32 [2, 32], P(None, 'col'), may hold values 0 or 1
Outputs:
- cross_block: float32 [1024, 2, 8192], P('col', None, 'row')
- child_block: float32 [1024, 2, 1024], P('row', None, 'col')
Inputs may be any that keep to these rules, and one draw needn't show every extreme that they name: top_inverse is symmetric. `child_inverse`: each child's block is zero above its diagonal: entry (k, i, j) is 0 where i < j. `tile_mask`: the pattern applied to the coupling block per tile of 256 top-separator rows.
All inputs are finite; a program needn't handle non-finite values.
Results may differ from a plain program's by a relative error of at most 0.00011.
Values sent between devices are 32-bit elements; how exact they have to be, the bound alone decides.
A program may use at most 64 MiB of HBM per device.

v0:
```python
import jax
import jax.numpy as jnp
from jax import lax
from jax.sharding import PartitionSpec as P

TILE = 256


def broadcast(value, axis, root):
    mine = lax.axis_index(axis) == root
    return lax.psum(jnp.where(mine, value, jnp.zeros_like(value)), axis)


def window(top_inverse, partial_value, inverse_rows):
    highest = lax.Precision.HIGHEST
    row_local = top_inverse.shape[0]
    col_local = top_inverse.shape[1]
    factor = lax.psum(partial_value, "row")
    offset_all = lax.axis_index("row") * row_local
    root_col = offset_all // col_local
    within = offset_all % col_local
    sent_rows = lax.dynamic_slice_in_dim(factor, within, row_local, 1)
    own_rows = broadcast(sent_rows, "col", root_col)
    image_share = lax.psum_scatter(
        jnp.einsum(
            "gjw,ij->wgi",
            factor,
            top_inverse,
            precision=highest,
            preferred_element_type=jnp.float32,
        ),
        "col",
        scatter_dimension=0,
        tiled=True,
    )
    col_share = image_share.shape[0]
    own_cols = lax.dynamic_slice_in_dim(
        inverse_rows, lax.axis_index("col") * col_share, col_share, 2
    )
    cross = jnp.einsum(
        "giw,vgi->wgv", own_rows, image_share, precision=highest, preferred_element_type=jnp.float32
    )
    gram = jnp.einsum(
        "gkw,gkv->wgv",
        inverse_rows,
        own_cols,
        precision=highest,
        preferred_element_type=jnp.float32,
    )
    child_share = lax.psum_scatter(cross + gram, "row", scatter_dimension=0, tiled=True)
    return (-image_share, child_share)


def local(top_inverse, coupling, child_inverse, tile_mask):
    mask_rows = jnp.repeat(tile_mask.astype(jnp.float32), TILE, axis=1)
    masked = coupling * mask_rows[:, :, None]
    partial_value = jnp.einsum(
        "ksc,kcw->ksw",
        masked,
        child_inverse,
        precision=lax.Precision.HIGHEST,
        preferred_element_type=jnp.float32,
    )
    lower_parts = []
    diag_parts = []
    for member in range(child_inverse.shape[0]):
        lower_block, diag_block = window(
            top_inverse, partial_value[member : member + 1], child_inverse[member : member + 1]
        )
        lower_parts.append(lower_block)
        diag_parts.append(diag_block)
    cross_block = jnp.concatenate(lower_parts, axis=1)
    child_block = jnp.concatenate(diag_parts, axis=1)
    return (cross_block, child_block)


def solution(mesh):
    in_specs = (P("row", "col"), P(None, "col", "row"), P(None, "row", None), P(None, "col"))
    out_specs = (P("col", None, "row"), P("row", None, "col"))
    return jax.shard_map(local, mesh=mesh, in_specs=in_specs, out_specs=out_specs, check_vma=False)
```

profile of v0, /device:TPU:1, one launch (start us, length us, event | category | flops | bytes accessed | tf_op | source)
XLA Modules:
  0.0 889.3 jit_solution(12631142725462969642)
XLA Ops:
  7.2 0.0 all-reduce.5.cloned.1.call-start
  7.2 0.7 convert_element_type.3
  8.0 0.1 broadcast_bitcast_fusion
  8.0 4.9 fusion.14
  12.9 2.3 fusion.27
  15.2 0.0 all-reduce.5.cloned.1.call-update
  15.2 0.0 all-reduce.7.cloned.1.call-start
  15.3 178.4 %all-reduce.5.cloned.1.call-done = (f32[1,512,1024]{2,1,0:T(8,128)}, f32[1,512,1024]{2,1,0:T(8,128)}) async-done(((f32[1,512,1024]{2,1,0:T(8,128)}, f32[1,512,1024]{2,1,0:T(8,128)}), (f32[1,512,1024]{2,1,0:T(8,128)}, f32[1,512,1024]{2,1,0:T(8,128)})) %all-reduce.5.cloned.1.call-update) | async-done | bytes 4194320 | tf_op jit(solution)/shard_map/psum | solution.py:18
  193.7 3.2 select_bitcast_fusion
  196.8 0.0 all-reduce.7.cloned.1.call-update
  196.9 0.0 reduce-scatter.7.cloned.1.call-start
  196.9 6.2 fusion.7
  203.2 0.0 reduce-scatter.5.cloned.1.call-start
  203.2 4.4 fusion.4
  207.6 0.0 reduce-scatter.5.cloned.1.call-update
  207.7 0.2 reduce-scatter.11.cloned.1.call-start
  207.9 1.3 fusion.28
  209.2 109.1 %all-reduce.7.cloned.1.call-done = (f32[256,1024]{1,0:T(8,128)}, f32[256,1024]{1,0:T(8,128)}) async-done(((f32[256,1024]{1,0:T(8,128)}, f32[256,1024]{1,0:T(8,128)}), (f32[256,1024]{1,0:T(8,128)}, f32[256,1024]{1,0:T(8,128)})) %all-reduce.7.cloned.1.call-update) | async-done | bytes 2097168 | tf_op jit(solution)/shard_map/psum | solution.py:11
  318.3 60.9 %reduce-scatter.7.cloned.1.call-done = f32[64,1,256]{2,0,1:T(8,128)} async-done(((f32[1024,1,256]{2,0,1:T(8,128)}), f32[64,1,256]{2,0,1:T(8,128)}) %reduce-scatter.7.cloned.1.call-update) | async-done | bytes 65552 | tf_op jit(solution)/shard_map/reduce_scatter | solution.py:24
  379.2 2.0 fusion.18
  381.2 0.5 fusion.10
  381.7 1.0 copy.9
  382.7 0.0 reduce-scatter.9.cloned.1.call-start
  382.8 57.8 %reduce-scatter.5.cloned.1.call-done = f32[64,1,256]{2,0,1:T(8,128)} async-done(((f32[1024,1,256]{2,0,1:T(8,128)}), f32[64,1,256]{2,0,1:T(8,128)}) %reduce-scatter.5.cloned.1.call-update) | async-done | bytes 65552 | tf_op jit(solution)/shard_map/reduce_scatter | solution.py:24
  440.6 1.7 fusion.21
  442.3 0.5 fusion.11
  442.8 1.0 copy.8
  443.8 0.0 reduce-scatter.9.cloned.1.call-update
  443.9 0.8 copy.10
  444.7 214.9 %reduce-scatter.11.cloned.1.call-done = f32[32,1,64]{2,1,0:T(1,128)} async-done(((f32[1024,1,64]{2,1,0:T(1,128)}), f32[32,1,64]{2,1,0:T(1,128)}) %reduce-scatter.11.cloned.1.call-update) | async-done | bytes 8208 | tf_op jit(solution)/shard_map/reduce_scatter | solution.py:50
  659.5 221.5 %reduce-scatter.9.cloned.1.call-done = f32[32,1,64]{2,1,0:T(1,128)} async-done(((f32[1024,1,64]{2,1,0:T(1,128)}), f32[32,1,64]{2,1,0:T(1,128)}) %reduce-scatter.9.cloned.1.call-update) | async-done | bytes 8208 | tf_op jit(solution)/shard_map/reduce_scatter | solution.py:50
  881.1 1.4 pad_maximum_fusion.1
  (16 shorter events, 0.1 us)
Async XLA Ops:
  7.2 189.8 %copy-start = (f32[256,512]{1,0:T(8,128)S(1)}, f32[256,512]{1,0:T(8,128)}, u32[]{:S(2)}) copy-start(f32[256,512]{1,0:T(8,128)} %param.4) | copy-start | bytes 1572868
  7.2 186.5 %all-reduce.5.cloned.1.call-start = ((), (), s32[]{:S(2)}) async-start(), calls=%async_computation.8 | async-start | bytes 8388608 | tf_op jit(solution)/shard_map/psum | solution.py:18
  15.2 303.1 %all-reduce.7.cloned.1.call-start = ((), (), s32[]{:S(2)}) async-start(), calls=%async_computation.9 | async-start | bytes 4194304 | tf_op jit(solution)/shard_map/psum | solution.py:11
  196.9 6.4 copy-start.1
  196.9 182.3 %reduce-scatter.7.cloned.1.call-start = ((), (), s32[]{:S(2)}) async-start(), calls=%async_computation.5 | async-start | bytes 1114112 | tf_op jit(solution)/shard_map/reduce_scatter | solution.py:24
  203.2 237.5 %reduce-scatter.5.cloned.1.call-start = ((), (), s32[]{:S(2)}) async-start(), calls=%async_computation.4 | async-start | bytes 1114112 | tf_op jit(solution)/shard_map/reduce_scatter | solution.py:24
  207.7 451.9 %reduce-scatter.11.cloned.1.call-start = ((), (), s32[]{:S(2)}) async-start(), calls=%async_computation.7 | async-start | bytes 540672 | tf_op jit(solution)/shard_map/reduce_scatter | solution.py:50
  318.3 122.4 %copy-start.2 = (f32[256,1024]{1,0:T(8,128)S(1)}, f32[256,1024]{1,0:T(8,128)}, u32[]{:S(2)}) copy-start(f32[256,1024]{1,0:T(8,128)} %get-tuple-element.9) | copy-start | bytes 3145732
  382.7 61.1 %copy-start.3 = (f32[64,1,256]{2,0,1:T(8,128)S(1)}, f32[64,1,256]{2,0,1:T(8,128)}, u32[]{:S(2)}) copy-start(f32[64,1,256]{2,0,1:T(8,128)} %reduce-scatter.7.cloned.1.call-done) | copy-start | bytes 196612
  382.7 498.3 %reduce-scatter.9.cloned.1.call-start = ((), (), s32[]{:S(2)}) async-start(), calls=%async_computation.6 | async-start | bytes 540672 | tf_op jit(solution)/shard_map/reduce_scatter | solution.py:50
  440.6 3.2 copy-start.4
Sparse Core Ops, SparseCore 0:
  15.3 178.3 all-reduce.4
  197.0 121.2 all-reduce.6
  321.3 57.8 reduce-scatter.6
  381.9 58.7 reduce-scatter.4
  445.5 213.9 reduce-scatter.10
  663.8 217.2 reduce-scatter.8
where the time goes:
time: 894 us; the launch traced here: 889 us
  waiting for transfers between devices  843 us (94%)
  matrix products  20.1 us (2%)
  between operations  14.2 us (2%)
    reduce_scatter x2, waiting for transfers between devices, window(): lax.psum_scatter(cross + gram, 'row', scatter_dimension=0, tiled=True)  436 us
    psum x1, waiting for transfers between devices, window(): factor = lax.psum(partial_value, 'row')  178 us
    reduce_scatter x2, waiting for transfers between devices, window(): lax.psum_scatter(jnp.einsum('gjw,ij->wgi', factor, top_inverse, precision...  119 us
    psum x1, waiting for transfers between devices, broadcast(): return lax.psum(jnp.where(mine, value, jnp.zeros_like(value)), axis)  109 us
  transfers between devices with their start and end apart: 6, of which 6 were waited for; matrix products, arithmetic and copies ran while one was open for 2% of the time, Pallas kernels for 0%

commit v1 on v0

v1 whole, which is shorter than its diff:
```python
import jax
import jax.numpy as jnp
from jax import lax
from jax.experimental import pallas as pl
from jax.experimental.pallas import tpu as pltpu
from jax.sharding import PartitionSpec as P

NX, NY, NZ = 4, 8, 8
MESH = pl.DeviceIdType.MESH
F32, BF16 = jnp.float32, jnp.bfloat16
NSEM = 160
EVEN = (4, 2, 6, 0)
ODD = (3, 5, 1, 7)


def split(value):
    high = value.astype(BF16)
    return high, (value - high.astype(F32)).astype(BF16)


def dot_nt(a, b):
    return lax.dot_general(a, b, (((1,), (1,)), ((), ())), preferred_element_type=F32)


def dot3(a_high, a_low, b_high, b_low):
    rows = a_high.shape[0]
    both = dot_nt(jnp.concatenate([a_high, a_low], axis=0), b_high)
    return both[:rows] + both[rows:] + dot_nt(a_high, b_low)


def kernel(
    top_ref, coupling_ref, inverse_ref, mask_ref, cross_ref, child_ref,
    xt, masked, xr, xz, cr, xth, xtl, tr, th, tl, pb, rb, fg, fy, fyh, fyl,
    acc, rd, img, neg, outr, ec, er, ch, chr_, gram, send_sem, recv_sem, last_sem,
):
    row, col = lax.axis_index("row"), lax.axis_index("col")
    x, y = lax.rem(row, NX), lax.div(row, NX)
    h, z = lax.rem(col, 2), lax.div(col, 2)
    k, half = lax.div(x, 2), lax.rem(x, 2)
    other = 1 - h
    parity = lax.rem(y + h, 2)
    own = 2 * h + half

    def at(px, py, pz, ph):
        return (py * NX + px, pz * 2 + ph)

    def xs(d):
        return lax.rem(x + d, NX)

    def ys(d):
        return lax.rem(y + d, NY)

    def zs(d):
        return lax.rem(z + d, NZ)

    started = []
    count = [0]

    def copy(src, dst, device, keep=True):
        i = count[0]
        count[0] += 1
        made = pltpu.make_async_remote_copy(
            src_ref=src, dst_ref=dst, send_sem=send_sem.at[i], recv_sem=recv_sem.at[i],
            device_id=device, device_id_type=MESH,
        )
        if keep:
            started.append(made)
        return made

    barrier = pltpu.get_barrier_semaphore()

    def greet(device):
        pl.semaphore_signal(barrier, inc=1, device_id=device, device_id_type=MESH)

    for d in range(1, NX):
        greet(at(xs(d), y, z, h))
        greet(at(xs(d), y, z, other))
    greet(at(x, y, z, other))
    for d in range(1, NY):
        greet(at(x, ys(d), z, h))
    greet(at(x, y, zs(1), h))
    greet(at(x, y, zs(7), h))

    @pl.when(y != z)
    def _():
        greet(at(x, z, y, h))

    for child in range(2):
        for s in range(8):
            xt[child, s] = inverse_ref[child, :, 128 * s : 128 * s + 128].T

    @pl.when(y != z)
    def _():
        pl.semaphore_wait(barrier, 17)

    @pl.when(y == z)
    def _():
        pl.semaphore_wait(barrier, 16)

    def x_rows(to_half, p):
        return pl.ds(pl.multiple_of(64 * h + 32 * to_half + 16 * p, 16), 16)

    x_copies = []
    for d in (1, 3, 2):
        to = xs(d)
        for p in range(2):
            made = copy(
                xt.at[lax.div(to, 2), :, x_rows(lax.rem(to, 2), p), :], xr.at[x, p], at(to, y, z, h)
            )
            made.start()
            x_copies.append(made)

    for child in range(2):
        for tile in range(2):
            number = mask_ref[child, tile].astype(F32)
            masked[child, 256 * tile : 256 * tile + 256] = (
                coupling_ref[child, 256 * tile : 256 * tile + 256] * number
            )

    def chunk_rows(s):
        dist = EVEN[s] + parity * (ODD[s] - EVEN[s])
        sub = lax.div(ys(dist), 2)
        return pl.ds(pl.multiple_of(128 * sub, 128), 128)

    c_copies = []
    for s in range(4):
        group = []
        for d in (1, 3, 2):
            to = xs(d)
            made = copy(
                masked.at[lax.div(to, 2), chunk_rows(s), :], cr.at[parity, s, x], at(to, y, z, h)
            )
            made.start()
            group.append(made)
        c_copies.append(group)
        cr[parity, s, x] = masked[k, chunk_rows(s), :]
    forwards = [
        copy(cr.at[parity, s], cr.at[parity, s], at(x, y, z, other)) for s in range(4)
    ]

    z_copies = []
    for d in (1, 3, 2):
        to = xs(d)
        made = copy(xt.at[lax.div(to, 2), z], xz.at[x], at(to, y, z, h))
        made.start()
        z_copies.append(made)
    xz[x] = xt[k, z]

    t_copies = []
    for d in (1, 3, 2):
        made = copy(top_ref, tr.at[h, x], at(xs(d), y, z, h))
        made.start()
        t_copies.append((d, made))
    t_forwards = [copy(top_ref, tr.at[h, x], at(x, y, z, other))]
    t_forwards[0].start()
    tr[h, x] = top_ref[...]

    for p in range(2):
        xr[x, p] = xt[k, :, x_rows(half, p), :]
    for made in x_copies:
        made.wait_recv()
    for p in range(2):
        for src in range(4):
            high, low = split(xr[src, p].reshape(128, 128))
            xth[128 * p : 128 * p + 128, 128 * src : 128 * src + 128] = high
            xtl[128 * p : 128 * p + 128, 128 * src : 128 * src + 128] = low

    def partial(which, s):
        @pl.when(parity == which)
        def _():
            for made in c_copies[s]:
                made.wait_recv()
            forwards[s].start()

        @pl.when(parity != which)
        def _():
            forwards[s].wait_recv()

        rows = jnp.concatenate([cr[which, s, src] for src in range(4)], axis=1)
        high, low = split(rows)
        return dot3(xth[...], xtl[...], high, low)

    up, down = at(x, ys(1), z, h), at(x, ys(7), z, h)
    pb[4] = partial(0, 0)
    prev_up = copy(pb.at[4, pl.ds(0, 128)], rb.at[0, 0, pl.ds(0, 128)], up)
    prev_down = copy(pb.at[4, pl.ds(128, 128)], rb.at[1, 0, pl.ds(128, 128)], down)
    prev_up.start()
    prev_down.start()
    pb[3] = partial(1, 0)
    pb[5] = partial(1, 1)
    for step in range(1, 4):
        prev_up.wait_recv()
        if step == 1:
            pb[3, :128] += rb[0, 0, :128]
        else:
            pb[4 - step] += rb[0, step - 1]
        prev_up = copy(pb.at[4 - step], rb.at[0, step], up)
        prev_up.start()
        prev_down.wait_recv()
        if step == 1:
            pb[5, 128:] += rb[1, 0, 128:]
        else:
            pb[4 + step] += rb[1, step - 1]
        prev_down = copy(pb.at[4 + step], rb.at[1, step], down)
        prev_down.start()
        if step == 1:
            pb[2] = partial(0, 1)
            pb[6] = partial(0, 2)
        if step == 2:
            pb[1] = partial(1, 2)
            pb[7] = partial(1, 3)
    pb[0] = partial(0, 3)

    for made in z_copies:
        made.wait_recv()
    high, low = split(jnp.concatenate([xz[src] for src in range(4)], axis=1))
    gram[...] = dot3(xth[...], xtl[...], high, low)

    prev_up.wait_recv()
    prev_down.wait_recv()
    fg[y] = (pb[0] + rb[0, 3] + rb[1, 3]).reshape(2, 128, 128)

    def ring_send(step, p):
        made = []
        for way, peer in ((0, up), (1, down)):
            index = ys(8 - step) if way == 0 else ys(step)
            if step < 3:
                ref = fg.at[index, p]
            else:
                ref = fg.at[index, p, pl.ds(64 * way, 64)]
            made.append(copy(ref, ref, peer))
            made[-1].start()
        return made

    ring = [ring_send(0, p) for p in range(2)]

    flip = copy(fg.at[y], fy.at[y], at(x, z, y, h), keep=False)

    @pl.when(y != z)
    def _():
        flip.start()

    @pl.when(y == z)
    def _():
        fy[z] = fg[y]

    def top_block(index):
        return lax.rem(index, 2), pl.ds(pl.multiple_of(128 * lax.div(index, 2), 128), 128)

    for step in range(1, 4):
        for p in range(2):
            for made in ring[p]:
                made.wait_recv()
            ring[p] = ring_send(step, p)
        d, made = t_copies[step - 1]
        made.wait_recv()
        ref = tr.at[h, xs(4 - d)]
        t_forwards.append(copy(ref, ref, at(x, y, z, other)))
        t_forwards[-1].start()
    for made in t_forwards:
        made.wait_recv()
    pairs = ((0, 4), (1, 7), (2, 6), (3, 5))
    for n, pair in enumerate(pairs):
        for side in range(2):
            core, lanes = top_block(ys(pair[side]))
            for src in range(4):
                high, low = split(tr[core, src, :, lanes])
                th[n, 256 * src : 256 * src + 256, 128 * side : 128 * side + 128] = high
                tl[n, 256 * src : 256 * src + 256, 128 * side : 128 * side + 128] = low

    front, back = at(x, y, zs(1), h), at(x, y, zs(7), h)

    def second_send(step):
        made = []
        for way, peer in ((0, front), (1, back)):
            index = zs(8 - step) if way == 0 else zs(step)
            ref = fy.at[index] if step < 3 else fy.at[index, way]
            made.append(copy(ref, ref, peer))
            made[-1].start()
        return made

    def image_part(p):
        for made in ring[p]:
            made.wait_recv()
        highs, lows = [], []
        for a, b in pairs:
            high, low = split(jnp.concatenate([fg[ys(a), p], fg[ys(b), p]], axis=1))
            highs.append(jnp.concatenate([high, low], axis=0))
            lows.append(high)
        for n in range(4):
            lanes = slice(256 * n, 256 * n + 256)
            total = None
            for i in range(4):
                both = dot_nt(highs[i], th[i, lanes, :])
                part = both[:128] + both[128:] + dot_nt(lows[i], tl[i, lanes, :])
                total = part if total is None else total + part
            acc[p, :, :, lanes] = total.reshape(8, 16, 256)

    def image_first(p):
        made = []
        for way, peer in ((0, front), (1, back)):
            made.append(
                copy(acc.at[p, zs(4), pl.ds(8 * way, 8)], rd.at[p, way, 0, pl.ds(8 * way, 8)], peer)
            )
            made[-1].start()
        return made

    def image_step(p, step, before):
        made = []
        for way, peer in ((0, front), (1, back)):
            before[way].wait_recv()
            index = zs(4 - step) if way == 0 else zs(4 + step)
            if step == 1:
                rows = pl.ds(8 * way, 8)
                acc[p, index, rows] += rd[p, way, 0, rows]
            else:
                acc[p, index] += rd[p, way, step - 1]
            made.append(copy(acc.at[p, index], rd.at[p, way, step], peer))
            made[-1].start()
        return made

    image_part(0)
    moving = [image_first(0), None]
    image_part(1)
    moving[1] = image_first(1)

    @pl.when(y != z)
    def _():
        flip.wait_recv()

    second = second_send(0)
    for step in range(1, 4):
        for p in range(2):
            moving[p] = image_step(p, step, moving[p])
        for made in second:
            made.wait_recv()
        second = second_send(step)

    image_copies, out_copies = [], []
    for p in range(2):
        for made in moving[p]:
            made.wait_recv()
        total = acc[p, z] + rd[p, 0, 3] + rd[p, 1, 3]
        img[own, p] = total
        neg[p] = -total
        for px, ph in ((lax.rem(x + 1 - 2 * half + NX, NX), h), (lax.rem(x + 1 - 2 * half + NX, NX), other), (x, other)):
            made = copy(img.at[own, p], img.at[own, p], at(px, y, z, ph))
            made.start()
            image_copies.append(made)
    for p in range(2):
        for d in (1, 3, 2):
            to = xs(d)
            lanes = pl.ds(pl.multiple_of(256 * to, 256), 256)
            made = copy(neg.at[p, :, lanes], outr.at[x, p], at(to, y, z, h))
            made.start()
            out_copies.append(made)
        outr[x, p] = neg[p, :, pl.ds(pl.multiple_of(256 * x, 256), 256)]

    for made in second:
        made.wait_recv()
    for c in range(8):
        block = 4 * (c % 2) + c // 2
        high, low = split(fy[c].reshape(256, 128))
        fyh[:, 128 * block : 128 * block + 128] = high
        fyl[:, 128 * block : 128 * block + 128] = low

    for made in image_copies:
        made.wait_recv()
    high, low = split(img[...].reshape(128, 1024))
    ec[...] = (gram[...] + dot3(fyh[...], fyl[...], high, low)).reshape(2, 8, 16, 128)
    e_copies = []
    for d in range(1, NY):
        made = copy(ec.at[:, ys(d)], er.at[d - 1], at(x, ys(d), z, h))
        made.start()
        e_copies.append(made)

    for made in out_copies:
        made.wait_recv()
    for src in range(4):
        for p in range(2):
            start = 32 * (src % 2) + 16 * p
            cross_ref[src // 2, start : start + 16] = outr[src, p]

    total = ec[:, y]
    for d in range(1, NY):
        e_copies[d - 1].wait_recv()
        total = total + er[d - 1]
    ch[...] = total.reshape(32, 128)

    def last(ph, sem):
        return pltpu.make_async_remote_copy(
            src_ref=ch, dst_ref=chr_.at[k], send_sem=last_sem.at[2 + sem], recv_sem=last_sem.at[k],
            device_id=at(own, y, z, ph), device_id_type=MESH,
        )

    last(other, 0).start()

    @pl.when(h != k)
    def _():
        last(h, 1).start()

    @pl.when(h == k)
    def _():
        chr_[k] = ch[...]

    def arrived(child):
        pltpu.make_async_remote_copy(
            src_ref=ch, dst_ref=chr_.at[child], send_sem=last_sem.at[2], recv_sem=last_sem.at[child],
            device_id=at(own, y, z, other), device_id_type=MESH,
        ).wait_recv()

    for child in range(2):
        @pl.when(jnp.logical_or(h != k, k != child))
        def _():
            arrived(child)

    @pl.when(h == 0)
    def _():
        child_ref[...] = chr_[:, :, :64]

    @pl.when(h == 1)
    def _():
        child_ref[...] = chr_[:, :, 64:]

    last(other, 0).wait_send()

    @pl.when(h != k)
    def _():
        last(h, 1).wait_send()

    @pl.when(y != z)
    def _():
        flip.wait_send()

    for made in started:
        made.wait_send()


def local(top_inverse, coupling, child_inverse, tile_mask):
    vmem = pl.BlockSpec(memory_space=pltpu.VMEM)
    scratch = [
        pltpu.VMEM((2, 8, 128, 128), F32),
        pltpu.VMEM((2, 512, 128), F32),
        pltpu.VMEM((4, 2, 8, 16, 128), F32),
        pltpu.VMEM((4, 128, 128), F32),
        pltpu.VMEM((2, 4, 4, 128, 128), F32),
        pltpu.VMEM((256, 512), BF16),
        pltpu.VMEM((256, 512), BF16),
        pltpu.VMEM((2, 4, 256, 512), F32),
        pltpu.VMEM((4, 1024, 256), BF16),
        pltpu.VMEM((4, 1024, 256), BF16),
        pltpu.VMEM((8, 256, 128), F32),
        pltpu.VMEM((2, 4, 256, 128), F32),
        pltpu.VMEM((8, 2, 128, 128), F32),
        pltpu.VMEM((8, 2, 128, 128), F32),
        pltpu.VMEM((256, 1024), BF16),
        pltpu.VMEM((256, 1024), BF16),
        pltpu.VMEM((2, 8, 16, 1024), F32),
        pltpu.VMEM((2, 2, 4, 16, 1024), F32),
        pltpu.VMEM((4, 2, 16, 1024), F32),
        pltpu.VMEM((2, 16, 1024), F32),
        pltpu.VMEM((4, 2, 16, 256), F32),
        pltpu.VMEM((2, 8, 16, 128), F32),
        pltpu.VMEM((7, 2, 16, 128), F32),
        pltpu.VMEM((32, 128), F32),
        pltpu.VMEM((2, 32, 128), F32),
        pltpu.VMEM((256, 128), F32),
        pltpu.SemaphoreType.DMA((NSEM,)),
        pltpu.SemaphoreType.DMA((NSEM,)),
        pltpu.SemaphoreType.DMA((4,)),
    ]
    cross, child = pl.pallas_call(
        kernel,
        out_shape=(
            jax.ShapeDtypeStruct((2, 64, 256), F32),
            jax.ShapeDtypeStruct((2, 32, 64), F32),
        ),
        in_specs=[vmem, vmem, vmem, pl.BlockSpec(memory_space=pltpu.SMEM)],
        out_specs=(vmem, vmem),
        scratch_shapes=scratch,
        compiler_params=pltpu.CompilerParams(
            collective_id=0, has_side_effects=True, vmem_limit_bytes=48 << 20
        ),
        name="selected_inverse",
    )(top_inverse, coupling, child_inverse, tile_mask)
    return jnp.transpose(cross, (1, 0, 2)), jnp.transpose(child, (1, 0, 2))


def solution(mesh):
    in_specs = (P("row", "col"), P(None, "col", "row"), P(None, "row", None), P(None, "col"))
    out_specs = (P("col", None, "row"), P("row", None, "col"))
    return jax.shard_map(local, mesh=mesh, in_specs=in_specs, out_specs=out_specs, check_vma=False)
```

time: 894 us -> 119 us (0.13)
  waiting for transfers between devices: 843 us -> 0 us
  Pallas kernels: 0 us -> 113 us
  matrix products: 20.1 us -> 0 us
  between operations: 14.2 us -> 0.65 us
    reduce_scatter x4 -> x0, waiting for transfers between devices: 555 us -> none  [the longest x2 436 us: window(): lax.psum_scatter(cross + gram, 'row', scatter_dimension=0, tiled=True)]
    psum x2 -> x0, waiting for transfers between devices: 287 us -> none  [the longest x1 178 us: window(): factor = lax.psum(partial_value, 'row')]
    pallas_call x0 -> x1, Pallas kernels: none -> 113 us  [local(): pl.pallas_call(kernel, out_shape=(jax.ShapeDtypeStruct((2, 64, 256), F32)...]
    dot_general x7 -> x0, matrix products: 20.1 us -> none  [the longest x2 10.6 us: window(): jnp.einsum('gjw,ij->wgi', factor, top_inverse, precision=highest, preferr...]
  transfers between devices with their start and end apart: 6 -> 0, of which waited for: 6 -> 0; matrix products, arithmetic and copies ran while one was open for 2% -> 0% of each run, Pallas kernels for 0% -> 0%
where the time goes in v1:
time: 119 us
  Pallas kernels  113 us (95%)
  local copies, waits for them, and re-layouts  5.38 us (5%)
    pallas_call x1, Pallas kernels, local(): pl.pallas_call(kernel, out_shape=(jax.ShapeDtypeStruct((2, 64, 256), F32)...  113 us
    unnamed x10, local copies, waits for them, and re-layouts  5.38 us

profile of v1, /device:TPU:1, one launch (start us, length us, event | category | flops | bytes accessed | tf_op | source)
XLA Modules:
  0.0 119.0 jit_solution(17982564158720063145)
XLA Ops:
  0.6 0.0 copy-start
  0.6 1.2 %copy-done = f32[2,128,1024]{2,1,0:T(8,128)S(1)} copy-done((f32[2,128,1024]{2,1,0:T(8,128)S(1)}, f32[2,128,1024]{2,1,0:T(8,128)}, u32[]{:S(2)}) %copy-start) | copy-done | bytes 1048600
  1.9 0.0 copy-start.1
  1.9 1.0 copy-done.1
  2.9 0.0 copy-start.2
  2.9 1.0 copy-done.2
  3.9 0.0 copy-start.3
  3.9 0.7 copy-done.3
  4.6 113.0 %selected_inverse.1 = (f32[2,64,256]{2,1,0:T(8,128)S(1)}, f32[2,32,64]{2,1,0:T(8,128)S(1)}) custom-call(f32[256,512]{1,0:T(8,128)S(1)} %copy-done.1, f32[2,512,128]{2,1,0:T(8,128)S(1)} %copy-done.2, f32[2,128,1024]{2,1,0:T(8,128)S(1)} %copy-done, s32[2,2]{1,0:T(2,128)S(1)} %copy-done.3), custom_call_target="tpu_custom_call" | custom-call | tf_op jit(solution)/shard_map/selected_inverse/pallas_call | solution.py:472
  117.6 0.8 copy.6
  118.3 0.6 copy.7
Async XLA Ops:
  0.6 1.2 %copy-start = (f32[2,128,1024]{2,1,0:T(8,128)S(1)}, f32[2,128,1024]{2,1,0:T(8,128)}, u32[]{:S(2)}) copy-start(f32[2,128,1024]{2,1,0:T(8,128)} %inverse_ref.1) | copy-start | bytes 3145732
  1.9 1.0 copy-start.1
  2.9 1.0 copy-start.2
  3.9 0.7 copy-start.3

commit v2 on v1

v2 whole, which is shorter than its diff:
```python
import jax
import jax.numpy as jnp
from jax import lax
from jax.experimental import pallas as pl
from jax.experimental.pallas import tpu as pltpu
from jax.sharding import PartitionSpec as P

NX, NY, NZ = 4, 8, 8
MESH = pl.DeviceIdType.MESH
F32, BF16 = jnp.float32, jnp.bfloat16
NSEM = 160
EVEN = (4, 2, 6, 0)
ODD = (3, 5, 1, 7)


def split(value):
    high = value.astype(BF16)
    return high, (value - high.astype(F32)).astype(BF16)


def dot_nt(a, b):
    return lax.dot_general(a, b, (((1,), (1,)), ((), ())), preferred_element_type=F32)


def dot3(a_high, a_low, b_high, b_low):
    rows = a_high.shape[0]
    both = dot_nt(jnp.concatenate([a_high, a_low], axis=0), b_high)
    return both[:rows] + both[rows:] + dot_nt(a_high, b_low)


def kernel(
    top_ref, coupling_ref, inverse_ref, mask_ref, cross_ref, child_ref,
    xin, xt, masked, xr, xz, cr, xb, tr, th, tl, pb, rb, fg, fy, fyh, fyl,
    acc, rd, img, neg, outr, ec, er, ch, chr_, gram, send_sem, recv_sem, last_sem, load_sem,
):
    row, col = lax.axis_index("row"), lax.axis_index("col")
    x, y = lax.rem(row, NX), lax.div(row, NX)
    h, z = lax.rem(col, 2), lax.div(col, 2)
    k, half = lax.div(x, 2), lax.rem(x, 2)
    other = 1 - h
    parity = lax.rem(y + h, 2)
    own = 2 * h + half

    def at(px, py, pz, ph):
        return (py * NX + px, pz * 2 + ph)

    def xs(d):
        return lax.rem(x + d, NX)

    def ys(d):
        return lax.rem(y + d, NY)

    def zs(d):
        return lax.rem(z + d, NZ)

    started = []
    count = [0]

    def copy(src, dst, device, keep=True):
        i = count[0]
        count[0] += 1
        made = pltpu.make_async_remote_copy(
            src_ref=src, dst_ref=dst, send_sem=send_sem.at[i], recv_sem=recv_sem.at[i],
            device_id=device, device_id_type=MESH,
        )
        if keep:
            started.append(made)
        return made

    loads = [
        pltpu.make_async_copy(inverse_ref, xin, load_sem.at[0]),
        pltpu.make_async_copy(coupling_ref, masked, load_sem.at[1]),
        pltpu.make_async_copy(top_ref, tr.at[h, x], load_sem.at[2]),
    ]
    for made in loads:
        made.start()
    barrier = pltpu.get_barrier_semaphore()

    def greet(device):
        pl.semaphore_signal(barrier, inc=1, device_id=device, device_id_type=MESH)

    for d in range(1, NX):
        greet(at(xs(d), y, z, h))
        greet(at(xs(d), y, z, other))
    greet(at(x, y, z, other))
    for d in range(1, NY):
        greet(at(x, ys(d), z, h))
    for d in (1, 2, 6, 7):
        greet(at(x, y, zs(d), h))

    @pl.when(y != z)
    def _():
        greet(at(x, z, y, h))

    loads[0].wait()
    for child in range(2):
        for s in range(8):
            xt[child, s] = xin[child, :, 128 * s : 128 * s + 128].T
    loads[1].wait()
    for child in range(2):
        for tile in range(2):
            number = mask_ref[child, tile].astype(F32)
            masked[child, 256 * tile : 256 * tile + 256] *= number

    @pl.when(y != z)
    def _():
        pl.semaphore_wait(barrier, 19)

    @pl.when(y == z)
    def _():
        pl.semaphore_wait(barrier, 18)

    def x_rows(to_half, p):
        return pl.ds(pl.multiple_of(64 * h + 32 * to_half + 16 * p, 16), 16)

    def x_send(p):
        made = []
        for d in (1, 3, 2):
            to = xs(d)
            made.append(
                copy(
                    xt.at[lax.div(to, 2), :, x_rows(lax.rem(to, 2), p), :],
                    xr.at[x, p],
                    at(to, y, z, h),
                )
            )
            made[-1].start()
        xr[x, p] = xt[k, :, x_rows(half, p), :]
        return made

    def chunk_rows(s):
        dist = EVEN[s] + parity * (ODD[s] - EVEN[s])
        sub = lax.div(ys(dist), 2)
        return pl.ds(pl.multiple_of(128 * sub, 128), 128)

    def c_send(s):
        made = []
        for d in (1, 3, 2):
            to = xs(d)
            made.append(
                copy(
                    masked.at[lax.div(to, 2), chunk_rows(s), :],
                    cr.at[parity, s, x],
                    at(to, y, z, h),
                )
            )
            made[-1].start()
        cr[parity, s, x] = masked[k, chunk_rows(s), :]
        return made

    x_copies = [x_send(0)]
    c_copies = [c_send(0)]
    x_copies.append(x_send(1))
    for s in range(1, 4):
        c_copies.append(c_send(s))
    forwards = [copy(cr.at[parity, s], cr.at[parity, s], at(x, y, z, other)) for s in range(4)]

    loads[2].wait()
    mine = tr.at[h, x]
    t_near = [copy(mine, mine, at(xs(d), y, z, h)) for d in (1, 3)]
    for made in t_near:
        made.start()
    t_cores = [copy(mine, mine, at(x, y, z, other))]
    t_cores[0].start()

    z_copies = []
    for d in (1, 3, 2):
        to = xs(d)
        made = copy(xt.at[lax.div(to, 2), z], xz.at[x], at(to, y, z, h))
        made.start()
        z_copies.append(made)
    xz[x] = xt[k, z]

    def convert(which, src):
        core = lax.rem(y + which, 2)
        rows = pl.ds(pl.multiple_of(256 * src, 256), 256)
        for i in range(2):
            n = which + 2 * i
            for side in range(2):
                far = lax.rem(8 - n, 8) if side else n
                dist = jnp.where(n == 0, 4 * side, far)
                lanes = pl.ds(pl.multiple_of(128 * lax.div(ys(dist), 2), 128), 128)
                high, low = split(tr[core, src, :, lanes])
                th[n, rows, 128 * side : 128 * side + 128] = high
                tl[n, rows, 128 * side : 128 * side + 128] = low

    def x_take(p):
        for made in x_copies[p]:
            made.wait_recv()
        for src in range(4):
            high, low = split(xr[src, p].reshape(128, 128))
            lanes = slice(128 * src, 128 * src + 128)
            xb[p, :128, lanes] = high
            xb[p, 128:, lanes] = low

    def take(which, s):
        @pl.when(parity == which)
        def _():
            for made in c_copies[s]:
                made.wait_recv()
            forwards[s].start()

        @pl.when(parity != which)
        def _():
            forwards[s].wait_recv()

        return split(jnp.concatenate([cr[which, s, src] for src in range(4)], axis=1))

    def partial(rows, p):
        high, low = rows
        both = dot_nt(xb[p], high)
        return both[:128] + both[128:] + dot_nt(xb[p, :128], low)

    def y_at(d):
        return at(x, ys(d), z, h)

    def sent(src, dst, device):
        made = copy(src, dst, device)
        made.start()
        return made

    near = (1, 7)
    over = (2, 6)
    x_take(0)
    rows4 = take(0, 0)
    first = [[None, None], [None, None]]
    moving = [[None, None], [None, None]]

    def far_factor(p):
        pb[4, p] = partial(rows4, p)
        for way in range(2):
            rows = pl.ds(64 * way, 64)
            first[p][way] = sent(pb.at[4, p, rows], rb.at[way, 0, p, rows], y_at(over[way]))

    def third_factor(rows, way, p):
        pb[3 + 2 * way, p] = partial(rows, p)
        moving[p][way] = sent(pb.at[3 + 2 * way, p], rb.at[way, 1, p], y_at(near[way]))

    far_factor(0)
    rows3 = take(1, 0)
    third_factor(rows3, 0, 0)
    rows5 = take(1, 1)
    third_factor(rows5, 1, 0)
    x_take(1)
    far_factor(1)
    third_factor(rows3, 0, 1)
    third_factor(rows5, 1, 1)
    for step in (2, 3):
        for way in range(2):
            slot = ((0, 1 + way), (1, 2 + way))[step - 2]
            rows = take(*slot)
            for p in range(2):
                pb[4 - step if way == 0 else 4 + step, p] = partial(rows, p)
        for p in range(2):
            for way in range(2):
                index = 4 - step if way == 0 else 4 + step
                moving[p][way].wait_recv()
                pb[index, p] += rb[way, step - 1, p]
                if step == 2:
                    first[p][way].wait_recv()
                    half_rows = slice(64 * way, 64 * way + 64)
                    pb[index, p, half_rows] += rb[way, 0, p, half_rows]
                moving[p][way] = sent(pb.at[index, p], rb.at[way, step, p], y_at(near[way]))
    rows0 = take(0, 3)
    for p in range(2):
        pb[0, p] = partial(rows0, p)
    convert(parity, x)

    def ring_send(p, step):
        made = []
        for way in range(2):
            index = ys((8 - step) % 8) if way == 0 else ys(step)
            if step == 2:
                ref = fg.at[index, p, pl.ds(64 * way, 64)]
                made.append(sent(ref, ref, y_at(over[way])))
            ref = fg.at[index, p]
            made.append(sent(ref, ref, y_at(near[way])))
        return made

    flips = [copy(fg.at[y, p], fy.at[y, p], at(x, z, y, h), keep=False) for p in range(2)]
    ring = [None, None]
    for p in range(2):
        for way in range(2):
            moving[p][way].wait_recv()
        fg[y, p] = pb[0, p] + rb[0, 3, p] + rb[1, 3, p]
        ring[p] = ring_send(p, 0)

    @pl.when(y != z)
    def _():
        for made in flips:
            made.start()

    @pl.when(y == z)
    def _():
        fy[z] = fg[y]

    for made in z_copies:
        made.wait_recv()
    high, low = split(jnp.concatenate([xz[src] for src in range(4)], axis=1))
    for p in range(2):
        gram[p] = partial((high, low), p)

    t_far = []
    for i in range(2):
        t_near[i].wait_recv()
        src = xs(3 - 2 * i)
        ref = tr.at[h, src, pl.ds(128 * i, 128)]
        t_far.append(sent(ref, ref, at(xs(1 + 2 * i), y, z, h)))
        ref = tr.at[h, src]
        t_cores.append(sent(ref, ref, at(x, y, z, other)))
    for p in range(2):
        for made in ring[p]:
            made.wait_recv()
        ring[p] = ring_send(p, 1)
    t_cores[0].wait_recv()
    convert(1 - parity, x)
    for i in range(2):
        convert(parity, xs(3 - 2 * i))
    for p in range(2):
        for made in ring[p]:
            made.wait_recv()
        ring[p] = ring_send(p, 2)

    def z_at(d):
        return at(x, y, zs(d), h)

    @pl.when(y != z)
    def _():
        for made in flips:
            made.wait_recv()

    second_near = [sent(fy.at[z], fy.at[z], z_at(near[way])) for way in range(2)]
    second_over = [sent(fy.at[z], fy.at[z], z_at(over[way])) for way in range(2)]
    for i in range(2):
        t_cores[1 + i].wait_recv()
        convert(1 - parity, xs(3 - 2 * i))
    t_last = []
    for i in range(2):
        t_far[i].wait_recv()
        ref = tr.at[h, xs(2), pl.ds(128 * i, 128)]
        t_last.append(sent(ref, ref, at(x, y, z, other)))
    convert(parity, xs(2))
    for made in t_last:
        made.wait_recv()
    convert(1 - parity, xs(2))

    pairs = ((0, 4), (1, 7), (2, 6), (3, 5))

    def image_part(p):
        for made in ring[p]:
            made.wait_recv()
        highs, lows = [], []
        for a, b in pairs:
            high, low = split(jnp.concatenate([fg[ys(a), p], fg[ys(b), p]], axis=1))
            highs.append(jnp.concatenate([high, low], axis=0))
            lows.append(high)
        for n in range(4):
            lanes = slice(256 * n, 256 * n + 256)
            total = None
            for i in range(4):
                both = dot_nt(highs[i], th[i, lanes, :])
                part = both[:128] + both[128:] + dot_nt(lows[i], tl[i, lanes, :])
                total = part if total is None else total + part
            acc[p, :, :, lanes] = total.reshape(8, 16, 256)

    def image_first(p):
        for way in range(2):
            rows = pl.ds(8 * way, 8)
            first[p][way] = sent(acc.at[p, zs(4), rows], rd.at[p, way, 0, rows], z_at(over[way]))
            moving[p][way] = sent(acc.at[p, zs(3 + 2 * way)], rd.at[p, way, 1], z_at(near[way]))

    def image_step(p, step):
        for way in range(2):
            index = zs(4 - step) if way == 0 else zs(4 + step)
            moving[p][way].wait_recv()
            acc[p, index] += rd[p, way, step - 1]
            if step == 2:
                first[p][way].wait_recv()
                rows = pl.ds(8 * way, 8)
                acc[p, index, rows] += rd[p, way, 0, rows]
            moving[p][way] = sent(acc.at[p, index], rd.at[p, way, step], z_at(near[way]))

    image_part(0)
    image_first(0)
    image_part(1)
    image_first(1)
    second_far = []
    for way in range(2):
        second_over[way].wait_recv()
        index = zs(6 - 4 * way)
        second_far.append(sent(fy.at[index], fy.at[index], z_at(near[way])))
        ref = fy.at[index, way]
        second_far.append(sent(ref, ref, z_at(over[way])))
    for step in (2, 3):
        for p in range(2):
            image_step(p, step)

    image_copies, out_copies = [], []
    for p in range(2):
        for made in moving[p]:
            made.wait_recv()
        total = acc[p, z] + rd[p, 0, 3] + rd[p, 1, 3]
        img[own, p] = total
        neg[p] = -total
        for px, ph in ((lax.rem(x + 1 - 2 * half + NX, NX), h), (lax.rem(x + 1 - 2 * half + NX, NX), other), (x, other)):
            made = copy(img.at[own, p], img.at[own, p], at(px, y, z, ph))
            made.start()
            image_copies.append(made)
    for p in range(2):
        for d in (1, 3, 2):
            to = xs(d)
            lanes = pl.ds(pl.multiple_of(256 * to, 256), 256)
            made = copy(neg.at[p, :, lanes], outr.at[x, p], at(to, y, z, h))
            made.start()
            out_copies.append(made)
        outr[x, p] = neg[p, :, pl.ds(pl.multiple_of(256 * x, 256), 256)]

    for made in second_near + second_far:
        made.wait_recv()
    for c in range(8):
        block = 4 * (c % 2) + c // 2
        high, low = split(fy[c].reshape(256, 128))
        fyh[:, 128 * block : 128 * block + 128] = high
        fyl[:, 128 * block : 128 * block + 128] = low

    for made in image_copies:
        made.wait_recv()
    high, low = split(img[...].reshape(128, 1024))
    ec[...] = (gram[...].reshape(256, 128) + dot3(fyh[...], fyl[...], high, low)).reshape(2, 8, 16, 128)
    e_copies = []
    for d in range(1, NY):
        made = copy(ec.at[:, ys(d)], er.at[d - 1], at(x, ys(d), z, h))
        made.start()
        e_copies.append(made)

    for made in out_copies:
        made.wait_recv()
    for src in range(4):
        for p in range(2):
            start = 32 * (src % 2) + 16 * p
            cross_ref[src // 2, start : start + 16] = outr[src, p]

    total = ec[:, y]
    for d in range(1, NY):
        e_copies[d - 1].wait_recv()
        total = total + er[d - 1]
    ch[...] = total.reshape(32, 128)

    def last(ph, sem):
        return pltpu.make_async_remote_copy(
            src_ref=ch, dst_ref=chr_.at[k], send_sem=last_sem.at[2 + sem], recv_sem=last_sem.at[k],
            device_id=at(own, y, z, ph), device_id_type=MESH,
        )

    last(other, 0).start()

    @pl.when(h != k)
    def _():
        last(h, 1).start()

    @pl.when(h == k)
    def _():
        chr_[k] = ch[...]

    def arrived(child):
        pltpu.make_async_remote_copy(
            src_ref=ch, dst_ref=chr_.at[child], send_sem=last_sem.at[2], recv_sem=last_sem.at[child],
            device_id=at(own, y, z, other), device_id_type=MESH,
        ).wait_recv()

    for child in range(2):
        @pl.when(jnp.logical_or(h != k, k != child))
        def _():
            arrived(child)

    @pl.when(h == 0)
    def _():
        child_ref[...] = chr_[:, :, :64]

    @pl.when(h == 1)
    def _():
        child_ref[...] = chr_[:, :, 64:]

    last(other, 0).wait_send()

    @pl.when(h != k)
    def _():
        last(h, 1).wait_send()

    @pl.when(y != z)
    def _():
        for made in flips:
            made.wait_send()

    for made in started:
        made.wait_send()


def local(top_inverse, coupling, child_inverse, tile_mask):
    vmem = pl.BlockSpec(memory_space=pltpu.VMEM)
    hbm = pl.BlockSpec(memory_space=pl.ANY)
    scratch = [
        pltpu.VMEM((2, 128, 1024), F32),
        pltpu.VMEM((2, 8, 128, 128), F32),
        pltpu.VMEM((2, 512, 128), F32),
        pltpu.VMEM((4, 2, 8, 16, 128), F32),
        pltpu.VMEM((4, 128, 128), F32),
        pltpu.VMEM((2, 4, 4, 128, 128), F32),
        pltpu.VMEM((2, 256, 512), BF16),
        pltpu.VMEM((2, 4, 256, 512), F32),
        pltpu.VMEM((4, 1024, 256), BF16),
        pltpu.VMEM((4, 1024, 256), BF16),
        pltpu.VMEM((8, 2, 128, 128), F32),
        pltpu.VMEM((2, 4, 2, 128, 128), F32),
        pltpu.VMEM((8, 2, 128, 128), F32),
        pltpu.VMEM((8, 2, 128, 128), F32),
        pltpu.VMEM((256, 1024), BF16),
        pltpu.VMEM((256, 1024), BF16),
        pltpu.VMEM((2, 8, 16, 1024), F32),
        pltpu.VMEM((2, 2, 4, 16, 1024), F32),
        pltpu.VMEM((4, 2, 16, 1024), F32),
        pltpu.VMEM((2, 16, 1024), F32),
        pltpu.VMEM((4, 2, 16, 256), F32),
        pltpu.VMEM((2, 8, 16, 128), F32),
        pltpu.VMEM((7, 2, 16, 128), F32),
        pltpu.VMEM((32, 128), F32),
        pltpu.VMEM((2, 32, 128), F32),
        pltpu.VMEM((2, 128, 128), F32),
        pltpu.SemaphoreType.DMA((NSEM,)),
        pltpu.SemaphoreType.DMA((NSEM,)),
        pltpu.SemaphoreType.DMA((4,)),
        pltpu.SemaphoreType.DMA((3,)),
    ]
    cross, child = pl.pallas_call(
        kernel,
        out_shape=(
            jax.ShapeDtypeStruct((2, 64, 256), F32),
            jax.ShapeDtypeStruct((2, 32, 64), F32),
        ),
        in_specs=[hbm, hbm, hbm, pl.BlockSpec(memory_space=pltpu.SMEM)],
        out_specs=(vmem, vmem),
        scratch_shapes=scratch,
        compiler_params=pltpu.CompilerParams(
            collective_id=0, has_side_effects=True, vmem_limit_bytes=48 << 20
        ),
        name="selected_inverse",
    )(top_inverse, coupling, child_inverse, tile_mask)
    return jnp.transpose(cross, (1, 0, 2)), jnp.transpose(child, (1, 0, 2))


def solution(mesh):
    in_specs = (P("row", "col"), P(None, "col", "row"), P(None, "row", None), P(None, "col"))
    out_specs = (P("col", None, "row"), P("row", None, "col"))
    return jax.shard_map(local, mesh=mesh, in_specs=in_specs, out_specs=out_specs, check_vma=False)
```

time: 119 us -> 113 us (0.950)
  Pallas kernels: 113 us -> 107 us
    pallas_call x1, Pallas kernels: 113 us -> 107 us  [local(): pl.pallas_call(kernel, out_shape=(jax.ShapeDtypeStruct((2, 64, 256), F32)...]
where the time goes in v2:
time: 113 us
  Pallas kernels  107 us (95%)
  local copies, waits for them, and re-layouts  5.38 us (5%)
    pallas_call x1, Pallas kernels, local(): pl.pallas_call(kernel, out_shape=(jax.ShapeDtypeStruct((2, 64, 256), F32)...  107 us
    unnamed x10, local copies, waits for them, and re-layouts  5.38 us

profile of v2, /device:TPU:1, one launch (start us, length us, event | category | flops | bytes accessed | tf_op | source)
XLA Modules:
  0.0 113.0 jit_solution(3789842469890894644)
XLA Ops:
  0.6 0.0 copy-start
  0.6 1.2 %copy-done = f32[2,128,1024]{2,1,0:T(8,128)S(1)} copy-done((f32[2,128,1024]{2,1,0:T(8,128)S(1)}, f32[2,128,1024]{2,1,0:T(8,128)}, u32[]{:S(2)}) %copy-start) | copy-done | bytes 1048600
  1.9 0.0 copy-start.1
  1.9 1.0 copy-done.1
  2.9 0.0 copy-start.2
  2.9 1.0 copy-done.2
  3.9 0.0 copy-start.3
  3.9 0.7 copy-done.3
  4.6 107.0 %selected_inverse.1 = (f32[2,64,256]{2,1,0:T(8,128)S(1)}, f32[2,32,64]{2,1,0:T(8,128)S(1)}) custom-call(f32[256,512]{1,0:T(8,128)S(1)} %copy-done.1, f32[2,512,128]{2,1,0:T(8,128)S(1)} %copy-done.2, f32[2,128,1024]{2,1,0:T(8,128)S(1)} %copy-done, s32[2,2]{1,0:T(2,128)S(1)} %copy-done.3), custom_call_target="tpu_custom_call" | custom-call | tf_op jit(solution)/shard_map/selected_inverse/pallas_call | solution.py:534
  111.6 0.8 copy.6
  112.4 0.6 copy.7
Async XLA Ops:
  0.6 1.2 %copy-start = (f32[2,128,1024]{2,1,0:T(8,128)S(1)}, f32[2,128,1024]{2,1,0:T(8,128)}, u32[]{:S(2)}) copy-start(f32[2,128,1024]{2,1,0:T(8,128)} %inverse_ref.1) | copy-start | bytes 3145732
  1.9 1.0 copy-start.1
  2.9 1.0 copy-start.2
  3.9 0.7 copy-start.3

commit v3 on v2

--- a/solution.py
+++ b/solution.py
@@ -4,6 +4,7 @@
 from jax.experimental import pallas as pl
 from jax.experimental.pallas import tpu as pltpu
 from jax.sharding import PartitionSpec as P
+
 
 NX, NY, NZ = 4, 8, 8
 MESH = pl.DeviceIdType.MESH
@@ -65,6 +66,11 @@
         )
         if keep:
             started.append(made)
+        return made
+
+    def sent(src, dst, device):
+        made = copy(src, dst, device)
+        made.start()
         return made
 
     loads = [
@@ -158,17 +164,14 @@
     loads[2].wait()
     mine = tr.at[h, x]
     t_near = [copy(mine, mine, at(xs(d), y, z, h)) for d in (1, 3)]
-    for made in t_near:
+    t_cores = [copy(mine, mine, at(x, y, z, other))]
+    for made in t_near + t_cores:
         made.start()
-    t_cores = [copy(mine, mine, at(x, y, z, other))]
-    t_cores[0].start()
 
     z_copies = []
     for d in (1, 3, 2):
         to = xs(d)
-        made = copy(xt.at[lax.div(to, 2), z], xz.at[x], at(to, y, z, h))
-        made.start()
-        z_copies.append(made)
+        z_copies.append(sent(xt.at[lax.div(to, 2), z], xz.at[x], at(to, y, z, h)))
     xz[x] = xt[k, z]
 
     def convert(which, src):
@@ -213,11 +216,6 @@
 
     def y_at(d):
         return at(x, ys(d), z, h)
-
-    def sent(src, dst, device):
-        made = copy(src, dst, device)
-        made.start()
-        return made
 
     near = (1, 7)
     over = (2, 6)
@@ -277,7 +275,27 @@
             made.append(sent(ref, ref, y_at(near[way])))
         return made
 
-    flips = [copy(fg.at[y, p], fy.at[y, p], at(x, z, y, h), keep=False) for p in range(2)]
+    flips, flip_sems = [], []
+    for p in range(2):
+        flip_sems.append(count[0])
+        flips.append(copy(fg.at[y, p], fy.at[y, p], at(x, z, y, h), keep=False))
+    relays = []
+
+    def relay(d, p):
+        i = count[0]
+        count[0] += 1
+        relays.append(
+            pltpu.make_async_remote_copy(
+                src_ref=fg.at[ys(d), p], dst_ref=fy.at[ys(d), p], send_sem=send_sem.at[i],
+                recv_sem=recv_sem.at[flip_sems[p]], device_id=at(x, y, zs(d), h),
+                device_id_type=MESH,
+            )
+        )
+
+        @pl.when(y == z)
+        def _():
+            relays[-1].start()
+
     ring = [None, None]
     for p in range(2):
         for way in range(2):
@@ -285,7 +303,12 @@
         fg[y, p] = pb[0, p] + rb[0, 3, p] + rb[1, 3, p]
         ring[p] = ring_send(p, 0)
 
-    @pl.when(y != z)
+    apart = lax.rem(z - y + 8, 8)
+    far_apart = y != z
+    for d in near:
+        far_apart = jnp.logical_and(far_apart, apart != d)
+
+    @pl.when(far_apart)
     def _():
         for made in flips:
             made.start()
@@ -312,6 +335,8 @@
         for made in ring[p]:
             made.wait_recv()
         ring[p] = ring_send(p, 1)
+        for d in near:
+            relay(d, p)
     t_cores[0].wait_recv()
     convert(1 - parity, x)
     for i in range(2):
@@ -329,8 +354,20 @@
         for made in flips:
             made.wait_recv()
 
-    second_near = [sent(fy.at[z], fy.at[z], z_at(near[way])) for way in range(2)]
-    second_over = [sent(fy.at[z], fy.at[z], z_at(over[way])) for way in range(2)]
+    def second_send(step):
+        made = []
+        for way in range(2):
+            index = zs((8 - step) % 8) if way == 0 else zs(step)
+            ref = fy.at[index, way] if step == 3 else fy.at[index]
+            made.append(sent(ref, ref, z_at(near[way])))
+        return made
+
+    def second_next(step):
+        for made in second[-1]:
+            made.wait_recv()
+        second.append(second_send(step))
+
+    second = [second_send(0)]
     for i in range(2):
         t_cores[1 + i].wait_recv()
         convert(1 - parity, xs(3 - 2 * i))
@@ -384,28 +421,23 @@
     image_first(0)
     image_part(1)
     image_first(1)
-    second_far = []
-    for way in range(2):
-        second_over[way].wait_recv()
-        index = zs(6 - 4 * way)
-        second_far.append(sent(fy.at[index], fy.at[index], z_at(near[way])))
-        ref = fy.at[index, way]
-        second_far.append(sent(ref, ref, z_at(over[way])))
     for step in (2, 3):
+        second_next(step - 1)
         for p in range(2):
             image_step(p, step)
-
-    image_copies, out_copies = [], []
+    second_next(3)
+
+    image_copies, image_cores, out_copies = [], [], []
     for p in range(2):
         for made in moving[p]:
             made.wait_recv()
         total = acc[p, z] + rd[p, 0, 3] + rd[p, 1, 3]
         img[own, p] = total
         neg[p] = -total
-        for px, ph in ((lax.rem(x + 1 - 2 * half + NX, NX), h), (lax.rem(x + 1 - 2 * half + NX, NX), other), (x, other)):
-            made = copy(img.at[own, p], img.at[own, p], at(px, y, z, ph))
-            made.start()
-            image_copies.append(made)
+        pair = lax.rem(x + 1 - 2 * half + NX, NX)
+        ref = img.at[own, p]
+        image_copies.append(sent(ref, ref, at(pair, y, z, h)))
+        image_cores.append(sent(ref, ref, at(x, y, z, other)))
     for p in range(2):
         for d in (1, 3, 2):
             to = xs(d)
@@ -415,7 +447,7 @@
             out_copies.append(made)
         outr[x, p] = neg[p, :, pl.ds(pl.multiple_of(256 * x, 256), 256)]
 
-    for made in second_near + second_far:
+    for made in second[-1]:
         made.wait_recv()
     for c in range(8):
         block = 4 * (c % 2) + c // 2
@@ -423,15 +455,17 @@
         fyh[:, 128 * block : 128 * block + 128] = high
         fyl[:, 128 * block : 128 * block + 128] = low
 
-    for made in image_copies:
+    for p in range(2):
+        image_copies[p].wait_recv()
+        ref = img.at[2 * h + 1 - half, p]
+        image_cores.append(sent(ref, ref, at(x, y, z, other)))
+    for made in image_cores:
         made.wait_recv()
     high, low = split(img[...].reshape(128, 1024))
     ec[...] = (gram[...].reshape(256, 128) + dot3(fyh[...], fyl[...], high, low)).reshape(2, 8, 16, 128)
     e_copies = []
-    for d in range(1, NY):
-        made = copy(ec.at[:, ys(d)], er.at[d - 1], at(x, ys(d), z, h))
-        made.start()
-        e_copies.append(made)
+    for d in (4, 3, 5, 2, 6, 1, 7):
+        e_copies.append(sent(ec.at[:, ys(d)], er.at[d - 1], y_at(d)))
 
     for made in out_copies:
         made.wait_recv()
@@ -440,9 +474,10 @@
             start = 32 * (src % 2) + 16 * p
             cross_ref[src // 2, start : start + 16] = outr[src, p]
 
+    for made in e_copies:
+        made.wait_recv()
     total = ec[:, y]
     for d in range(1, NY):
-        e_copies[d - 1].wait_recv()
         total = total + er[d - 1]
     ch[...] = total.reshape(32, 128)
 
@@ -487,18 +522,23 @@
     def _():
         last(h, 1).wait_send()
 
-    @pl.when(y != z)
+    @pl.when(far_apart)
     def _():
         for made in flips:
             made.wait_send()
 
+    @pl.when(y == z)
+    def _():
+        for made in relays:
+            made.wait_send()
+
     for made in started:
         made.wait_send()
 
 
 def local(top_inverse, coupling, child_inverse, tile_mask):
     vmem = pl.BlockSpec(memory_space=pltpu.VMEM)
-    hbm = pl.BlockSpec(memory_space=pl.ANY)
+    hbm = pl.BlockSpec(memory_space=pltpu.HBM)
     scratch = [
         pltpu.VMEM((2, 128, 1024), F32),
         pltpu.VMEM((2, 8, 128, 128), F32),
@@ -541,7 +581,7 @@
         out_specs=(vmem, vmem),
         scratch_shapes=scratch,
         compiler_params=pltpu.CompilerParams(
-            collective_id=0, has_side_effects=True, vmem_limit_bytes=48 << 20
+            collective_id=0, has_side_effects=True, vmem_limit_bytes=60 << 20
         ),
         name="selected_inverse",
     )(top_inverse, coupling, child_inverse, tile_mask)

time: 113 us -> 103 us (0.912)
  Pallas kernels: 107 us -> 100 us
  local copies, waits for them, and re-layouts: 5.38 us -> 2.31 us
    pallas_call x1, Pallas kernels: 107 us -> 100 us  [local(): pl.pallas_call(kernel, out_shape=(jax.ShapeDtypeStruct((2, 64, 256), F32)...]
    unnamed x10 -> x4, local copies, waits for them, and re-layouts: 5.38 us -> 2.31 us
where the time goes in v3:
time: 103 us
  Pallas kernels  100 us (97%)
  local copies, waits for them, and re-layouts  2.31 us (2%)
    pallas_call x1, Pallas kernels, local(): pl.pallas_call(kernel, out_shape=(jax.ShapeDtypeStruct((2, 64, 256), F32)...  100 us
    unnamed x4, local copies, waits for them, and re-layouts  2.31 us

profile of v3, /device:TPU:1, one launch (start us, length us, event | category | flops | bytes accessed | tf_op | source)
XLA Modules:
  0.0 102.9 jit_solution(4325214784092565122)
XLA Ops:
  0.6 100.0 %selected_inverse.1 = (f32[2,64,256]{2,1,0:T(8,128)}, f32[2,32,64]{2,1,0:T(8,128)}) custom-call(f32[256,512]{1,0:T(8,128)} %top_ref.1, f32[2,512,128]{2,1,0:T(8,128)} %coupling_ref.1, f32[2,128,1024]{2,1,0:T(8,128)} %inverse_ref.1, s32[2,2]{1,0:T(2,128)} %mask_ref.1), custom_call_target="tpu_custom_call" | custom-call | tf_op jit(solution)/shard_map/selected_inverse/pallas_call | solution.py:574
  100.6 0.0 copy-start
  100.6 1.7 %copy.6 = f32[64,2,256]{2,1,0:T(2,128)} copy(f32[64,2,256]{2,0,1:T(8,128)} %bitcast.2) | data formatting | bytes 262144
  102.3 0.0 copy-done
  102.3 0.6 copy.7
Async XLA Ops:
  100.6 1.7 %copy-start = (f32[2,32,64]{2,1,0:T(8,128)S(1)}, f32[2,32,64]{2,1,0:T(8,128)}, u32[]{:S(2)}) copy-start(f32[2,32,64]{2,1,0:T(8,128)} %get-tuple-element.5) | copy-start | bytes 49156

commit v4 on v3

--- a/solution.py
+++ b/solution.py
@@ -32,7 +32,7 @@
 def kernel(
     top_ref, coupling_ref, inverse_ref, mask_ref, cross_ref, child_ref,
     xin, xt, masked, xr, xz, cr, xb, tr, th, tl, pb, rb, fg, fy, fyh, fyl,
-    acc, rd, img, neg, outr, ec, er, ch, chr_, gram, send_sem, recv_sem, last_sem, load_sem,
+    acc, rd, img, neg, outr, ec, er, gram, send_sem, recv_sem, last_sem, load_sem,
 ):
     row, col = lax.axis_index("row"), lax.axis_index("col")
     x, y = lax.rem(row, NX), lax.div(row, NX)
@@ -74,8 +74,8 @@
         return made
 
     loads = [
-        pltpu.make_async_copy(inverse_ref, xin, load_sem.at[0]),
-        pltpu.make_async_copy(coupling_ref, masked, load_sem.at[1]),
+        pltpu.make_async_copy(coupling_ref, masked, load_sem.at[0]),
+        pltpu.make_async_copy(inverse_ref, xin, load_sem.at[1]),
         pltpu.make_async_copy(top_ref, tr.at[h, x], load_sem.at[2]),
     ]
     for made in loads:
@@ -89,8 +89,11 @@
         greet(at(xs(d), y, z, h))
         greet(at(xs(d), y, z, other))
     greet(at(x, y, z, other))
+    for d in (1, 2, 6, 7):
+        greet(at(x, ys(d), z, h))
     for d in range(1, NY):
-        greet(at(x, ys(d), z, h))
+        for child in range(2):
+            greet(at(2 * child + half, ys(d), z, k))
     for d in (1, 2, 6, 7):
         greet(at(x, y, zs(d), h))
 
@@ -99,10 +102,6 @@
         greet(at(x, z, y, h))
 
     loads[0].wait()
-    for child in range(2):
-        for s in range(8):
-            xt[child, s] = xin[child, :, 128 * s : 128 * s + 128].T
-    loads[1].wait()
     for child in range(2):
         for tile in range(2):
             number = mask_ref[child, tile].astype(F32)
@@ -110,11 +109,11 @@
 
     @pl.when(y != z)
     def _():
-        pl.semaphore_wait(barrier, 19)
+        pl.semaphore_wait(barrier, 30)
 
     @pl.when(y == z)
     def _():
-        pl.semaphore_wait(barrier, 18)
+        pl.semaphore_wait(barrier, 29)
 
     def x_rows(to_half, p):
         return pl.ds(pl.multiple_of(64 * h + 32 * to_half + 16 * p, 16), 16)
@@ -154,9 +153,12 @@
         cr[parity, s, x] = masked[k, chunk_rows(s), :]
         return made
 
-    x_copies = [x_send(0)]
     c_copies = [c_send(0)]
-    x_copies.append(x_send(1))
+    loads[1].wait()
+    for child in range(2):
+        for s in range(8):
+            xt[child, s] = xin[child, :, 128 * s : 128 * s + 128].T
+    x_copies = [x_send(0), x_send(1)]
     for s in range(1, 4):
         c_copies.append(c_send(s))
     forwards = [copy(cr.at[parity, s], cr.at[parity, s], at(x, y, z, other)) for s in range(4)]
@@ -244,12 +246,13 @@
     third_factor(rows3, 0, 1)
     third_factor(rows5, 1, 1)
     for step in (2, 3):
+        taken = []
         for way in range(2):
             slot = ((0, 1 + way), (1, 2 + way))[step - 2]
-            rows = take(*slot)
-            for p in range(2):
-                pb[4 - step if way == 0 else 4 + step, p] = partial(rows, p)
+            taken.append(take(*slot))
         for p in range(2):
+            for way in range(2):
+                pb[4 - step if way == 0 else 4 + step, p] = partial(taken[way], p)
             for way in range(2):
                 index = 4 - step if way == 0 else 4 + step
                 moving[p][way].wait_recv()
@@ -305,7 +308,7 @@
 
     apart = lax.rem(z - y + 8, 8)
     far_apart = y != z
-    for d in near:
+    for d in near + over:
         far_apart = jnp.logical_and(far_apart, apart != d)
 
     @pl.when(far_apart)
@@ -345,6 +348,8 @@
         for made in ring[p]:
             made.wait_recv()
         ring[p] = ring_send(p, 2)
+        for d in over:
+            relay(d, p)
 
     def z_at(d):
         return at(x, y, zs(d), h)
@@ -462,10 +467,31 @@
     for made in image_cores:
         made.wait_recv()
     high, low = split(img[...].reshape(128, 1024))
-    ec[...] = (gram[...].reshape(256, 128) + dot3(fyh[...], fyl[...], high, low)).reshape(2, 8, 16, 128)
-    e_copies = []
-    for d in (4, 3, 5, 2, 6, 1, 7):
-        e_copies.append(sent(ec.at[:, ys(d)], er.at[d - 1], y_at(d)))
+    total = gram[...].reshape(256, 128) + dot3(fyh[...], fyl[...], high, low)
+    total = total.reshape(2, 8, 16, 128)
+    for ph in range(2):
+        lanes = slice(64 * ph, 64 * ph + 64)
+        ec[ph] = jnp.concatenate([total[0, :, :, lanes], total[1, :, :, lanes]], axis=-1)
+
+    def last(d, ph, i):
+        return pltpu.make_async_remote_copy(
+            src_ref=ec.at[ph, ys(d)], dst_ref=er.at[k, d], send_sem=last_sem.at[16 + i],
+            recv_sem=last_sem.at[8 * k + d], device_id=at(own, ys(d), z, ph), device_id_type=MESH,
+        )
+
+    order = (4, 3, 5, 2, 6, 1, 7, 0)
+    for d in order:
+        last(d, other, 8 + d).start()
+        if d:
+            last(d, h, d).start()
+
+    @pl.when(h != k)
+    def _():
+        last(0, h, 0).start()
+
+    @pl.when(h == k)
+    def _():
+        er[k, 0] = ec[h, y]
 
     for made in out_copies:
         made.wait_recv()
@@ -474,53 +500,35 @@
             start = 32 * (src % 2) + 16 * p
             cross_ref[src // 2, start : start + 16] = outr[src, p]
 
-    for made in e_copies:
-        made.wait_recv()
-    total = ec[:, y]
-    for d in range(1, NY):
-        total = total + er[d - 1]
-    ch[...] = total.reshape(32, 128)
-
-    def last(ph, sem):
-        return pltpu.make_async_remote_copy(
-            src_ref=ch, dst_ref=chr_.at[k], send_sem=last_sem.at[2 + sem], recv_sem=last_sem.at[k],
-            device_id=at(own, y, z, ph), device_id_type=MESH,
-        )
-
-    last(other, 0).start()
-
-    @pl.when(h != k)
-    def _():
-        last(h, 1).start()
-
-    @pl.when(h == k)
-    def _():
-        chr_[k] = ch[...]
-
-    def arrived(child):
+    def arrived(child, d):
         pltpu.make_async_remote_copy(
-            src_ref=ch, dst_ref=chr_.at[child], send_sem=last_sem.at[2], recv_sem=last_sem.at[child],
-            device_id=at(own, y, z, other), device_id_type=MESH,
+            src_ref=ec.at[0, 0], dst_ref=er.at[child, d], send_sem=last_sem.at[16],
+            recv_sem=last_sem.at[8 * child + d], device_id=at(own, y, z, other),
+            device_id_type=MESH,
         ).wait_recv()
 
     for child in range(2):
+        for d in range(1, NY):
+            arrived(child, d)
+
         @pl.when(jnp.logical_or(h != k, k != child))
         def _():
-            arrived(child)
-
-    @pl.when(h == 0)
-    def _():
-        child_ref[...] = chr_[:, :, :64]
-
-    @pl.when(h == 1)
-    def _():
-        child_ref[...] = chr_[:, :, 64:]
-
-    last(other, 0).wait_send()
+            arrived(child, 0)
+
+        total = er[child, 0]
+        for d in range(1, NY):
+            total = total + er[child, d]
+        child_ref[child, :16] = total[:, :64]
+        child_ref[child, 16:] = total[:, 64:]
+
+    for d in order:
+        last(d, other, 8 + d).wait_send()
+        if d:
+            last(d, h, d).wait_send()
 
     @pl.when(h != k)
     def _():
-        last(h, 1).wait_send()
+        last(0, h, 0).wait_send()
 
     @pl.when(far_apart)
     def _():
@@ -562,13 +570,11 @@
         pltpu.VMEM((2, 16, 1024), F32),
         pltpu.VMEM((4, 2, 16, 256), F32),
         pltpu.VMEM((2, 8, 16, 128), F32),
-        pltpu.VMEM((7, 2, 16, 128), F32),
-        pltpu.VMEM((32, 128), F32),
-        pltpu.VMEM((2, 32, 128), F32),
+        pltpu.VMEM((2, 8, 16, 128), F32),
         pltpu.VMEM((2, 128, 128), F32),
         pltpu.SemaphoreType.DMA((NSEM,)),
         pltpu.SemaphoreType.DMA((NSEM,)),
-        pltpu.SemaphoreType.DMA((4,)),
+        pltpu.SemaphoreType.DMA((32,)),
         pltpu.SemaphoreType.DMA((3,)),
     ]
     cross, child = pl.pallas_call(

time: 103 us -> 102 us (level)
  no operation moved by 1% of the time
where the time goes in v4:
time: 102 us
  Pallas kernels  99.3 us (97%)
  local copies, waits for them, and re-layouts  2.31 us (2%)
    pallas_call x1, Pallas kernels, local(): pl.pallas_call(kernel, out_shape=(jax.ShapeDtypeStruct((2, 64, 256), F32)...  99.3 us
    unnamed x4, local copies, waits for them, and re-layouts  2.31 us

profile of v4, /device:TPU:1, one launch (start us, length us, event | category | flops | bytes accessed | tf_op | source)
XLA Modules:
  0.0 102.3 jit_solution(14588844830885343315)
XLA Ops:
  0.6 99.3 %selected_inverse.1 = (f32[2,64,256]{2,1,0:T(8,128)}, f32[2,32,64]{2,1,0:T(8,128)}) custom-call(f32[256,512]{1,0:T(8,128)} %top_ref.1, f32[2,512,128]{2,1,0:T(8,128)} %coupling_ref.1, f32[2,128,1024]{2,1,0:T(8,128)} %inverse_ref.1, s32[2,2]{1,0:T(2,128)} %mask_ref.1), custom_call_target="tpu_custom_call" | custom-call | tf_op jit(solution)/shard_map/selected_inverse/pallas_call | solution.py:580
  100.0 0.0 copy-start
  100.0 1.7 %copy.6 = f32[64,2,256]{2,1,0:T(2,128)} copy(f32[64,2,256]{2,0,1:T(8,128)} %bitcast.2) | data formatting | bytes 262144
  101.7 0.0 copy-done
  101.7 0.6 copy.7
Async XLA Ops:
  100.0 1.7 %copy-start = (f32[2,32,64]{2,1,0:T(8,128)S(1)}, f32[2,32,64]{2,1,0:T(8,128)}, u32[]{:S(2)}) copy-start(f32[2,32,64]{2,1,0:T(8,128)} %get-tuple-element.5) | copy-start | bytes 49156

commit v5 on v4

--- a/solution.py
+++ b/solution.py
@@ -299,22 +299,23 @@
         def _():
             relays[-1].start()
 
+    apart = lax.rem(z - y + 8, 8)
+    far_apart = y != z
+    for d in near + over:
+        far_apart = jnp.logical_and(far_apart, apart != d)
+
+    def flip_start(made):
+        @pl.when(far_apart)
+        def _():
+            made.start()
+
     ring = [None, None]
     for p in range(2):
         for way in range(2):
             moving[p][way].wait_recv()
         fg[y, p] = pb[0, p] + rb[0, 3, p] + rb[1, 3, p]
         ring[p] = ring_send(p, 0)
-
-    apart = lax.rem(z - y + 8, 8)
-    far_apart = y != z
-    for d in near + over:
-        far_apart = jnp.logical_and(far_apart, apart != d)
-
-    @pl.when(far_apart)
-    def _():
-        for made in flips:
-            made.start()
+        flip_start(flips[p])
 
     @pl.when(y == z)
     def _():

time: 102 us -> 102 us (level)
  no operation moved by 1% of the time
where the time goes in v5:
time: 102 us
  Pallas kernels  98.9 us (97%)
  local copies, waits for them, and re-layouts  2.31 us (2%)
    pallas_call x1, Pallas kernels, local(): pl.pallas_call(kernel, out_shape=(jax.ShapeDtypeStruct((2, 64, 256), F32)...  98.9 us
    unnamed x4, local copies, waits for them, and re-layouts  2.31 us

profile of v5, /device:TPU:1, one launch (start us, length us, event | category | flops | bytes accessed | tf_op | source)
XLA Modules:
  0.0 101.9 jit_solution(9338137212423596425)
XLA Ops:
  0.6 98.9 %selected_inverse.1 = (f32[2,64,256]{2,1,0:T(8,128)}, f32[2,32,64]{2,1,0:T(8,128)}) custom-call(f32[256,512]{1,0:T(8,128)} %top_ref.1, f32[2,512,128]{2,1,0:T(8,128)} %coupling_ref.1, f32[2,128,1024]{2,1,0:T(8,128)} %inverse_ref.1, s32[2,2]{1,0:T(2,128)} %mask_ref.1), custom_call_target="tpu_custom_call" | custom-call | tf_op jit(solution)/shard_map/selected_inverse/pallas_call | solution.py:581
  99.5 0.0 copy-start
  99.6 1.7 %copy.6 = f32[64,2,256]{2,1,0:T(2,128)} copy(f32[64,2,256]{2,0,1:T(8,128)} %bitcast.2) | data formatting | bytes 262144
  101.2 0.0 copy-done
  101.2 0.6 copy.7
Async XLA Ops:
  99.5 1.7 %copy-start = (f32[2,32,64]{2,1,0:T(8,128)S(1)}, f32[2,32,64]{2,1,0:T(8,128)}, u32[]{:S(2)}) copy-start(f32[2,32,64]{2,1,0:T(8,128)} %get-tuple-element.5) | copy-start | bytes 49156

commit v6 on v5

--- a/solution.py
+++ b/solution.py
@@ -198,12 +198,16 @@
             xb[p, :128, lanes] = high
             xb[p, 128:, lanes] = low
 
+    def push(s):
+        for made in c_copies[s]:
+            made.wait_recv()
+        forwards[s].start()
+
     def take(which, s):
-        @pl.when(parity == which)
-        def _():
-            for made in c_copies[s]:
-                made.wait_recv()
-            forwards[s].start()
+        if s:
+            @pl.when(parity == which)
+            def _():
+                push(s)
 
         @pl.when(parity != which)
         def _():
@@ -221,6 +225,7 @@
 
     near = (1, 7)
     over = (2, 6)
+    push(0)
     x_take(0)
     rows4 = take(0, 0)
     first = [[None, None], [None, None]]
@@ -453,6 +458,10 @@
             out_copies.append(made)
         outr[x, p] = neg[p, :, pl.ds(pl.multiple_of(256 * x, 256), 256)]
 
+    for p in range(2):
+        image_copies[p].wait_recv()
+        ref = img.at[2 * h + 1 - half, p]
+        image_cores.append(sent(ref, ref, at(x, y, z, other)))
     for made in second[-1]:
         made.wait_recv()
     for c in range(8):
@@ -461,10 +470,6 @@
         fyh[:, 128 * block : 128 * block + 128] = high
         fyl[:, 128 * block : 128 * block + 128] = low
 
-    for p in range(2):
-        image_copies[p].wait_recv()
-        ref = img.at[2 * h + 1 - half, p]
-        image_cores.append(sent(ref, ref, at(x, y, z, other)))
     for made in image_cores:
         made.wait_recv()
     high, low = split(img[...].reshape(128, 1024))

time: 102 us -> 102 us (level)
  no operation moved by 1% of the time
where the time goes in v6:
time: 102 us
  Pallas kernels  98.9 us (97%)
  local copies, waits for them, and re-layouts  2.31 us (2%)
    pallas_call x1, Pallas kernels, local(): pl.pallas_call(kernel, out_shape=(jax.ShapeDtypeStruct((2, 64, 256), F32)...  98.9 us
    unnamed x4, local copies, waits for them, and re-layouts  2.31 us

profile of v6, /device:TPU:1, one launch (start us, length us, event | category | flops | bytes accessed | tf_op | source)
XLA Modules:
  0.0 101.8 jit_solution(12582546946934970662)
XLA Ops:
  0.6 98.9 %selected_inverse.1 = (f32[2,64,256]{2,1,0:T(8,128)}, f32[2,32,64]{2,1,0:T(8,128)}) custom-call(f32[256,512]{1,0:T(8,128)} %top_ref.1, f32[2,512,128]{2,1,0:T(8,128)} %coupling_ref.1, f32[2,128,1024]{2,1,0:T(8,128)} %inverse_ref.1, s32[2,2]{1,0:T(2,128)} %mask_ref.1), custom_call_target="tpu_custom_call" | custom-call | tf_op jit(solution)/shard_map/selected_inverse/pallas_call | solution.py:586
  99.5 0.0 copy-start
  99.5 1.7 %copy.6 = f32[64,2,256]{2,1,0:T(2,128)} copy(f32[64,2,256]{2,0,1:T(8,128)} %bitcast.2) | data formatting | bytes 262144
  101.2 0.0 copy-done
  101.2 0.6 copy.7
Async XLA Ops:
  99.5 1.7 %copy-start = (f32[2,32,64]{2,1,0:T(8,128)S(1)}, f32[2,32,64]{2,1,0:T(8,128)}, u32[]{:S(2)}) copy-start(f32[2,32,64]{2,1,0:T(8,128)} %get-tuple-element.5) | copy-start | bytes 49156
